TPU v7x, 128 devices: a whole 4x4x4 slice. The times are simulated.
128 devices in a mesh: face: 4 (over x), tile: 32 (over z, y, core).
Axes of the slice: x: 4, y: 4, z: 4, core: 2. Of those that a mesh axis runs over, the one named last changes fastest.
Arguments:
- squeeze_anomaly: float32 [8, 32, 4096], P(None, 'face', 'tile'), may hold values from -6 to 6
- eastward_airflow: float32 [8, 32, 4096], P(None, 'face', 'tile'), may hold values from -6 to 6
- northward_airflow: float32 [8, 32, 4096], P(None, 'face', 'tile'), may hold values from -6 to 6
- thermal_anomaly: float32 [8, 32, 4096], P(None, 'face', 'tile'), may hold values from -6 to 6
- diffusivity_link: float32 [8, 32, 4096], P(None, 'face', 'tile'), may hold values from 0.1 to 4
- sound_stability_ratio: float32 [8], replicated, may hold values from 0.1 to 0.3
- overlay_source_site: int32 [128, 128, 128], P(('face', 'tile')), may hold values from 0 to 1023
- overlay_target_floe: int32 [128, 128, 128], P(('face', 'tile')), may hold values from 0 to 2047
- overlay_fraction: float32 [128, 128, 128], P(('face', 'tile')), may hold values from 0 to 1, as said below
- floe_skin_kelvin: float32 [262144], P(('face', 'tile')), may hold values from -6 to 6
- frozen_indicator: int32 [262144], P(('face', 'tile')), may hold values 0 or 1
- floe_motion: float32 [262144], P(('face', 'tile')), may hold values from -4 to 4
- floe_strain_tensor: float32 [262144], P(('face', 'tile')), may hold values from -4 to 4
- floe_compress_resist: float32 [262144], P(('face', 'tile')), may hold values from 0.5 to 2
Outputs:
- temp_new: float32 [8, 32, 4096], P(None, 'face', 'tile')
- pressure_new: float32 [8, 32, 4096], P(None, 'face', 'tile')
- floe_skin_fresh: float32 [262144], P(('face', 'tile'))
- ice_velocity_new: float32 [262144], P(('face', 'tile'))
Inputs may be any that keep to these rules, and one draw needn't show every extreme that they name: `overlay_fraction`: A slot with area 0 is empty; for each pair of devices the live slots come first; in every draw some destination devices receive 128 live slots from every source.
All inputs are finite; a program needn't handle non-finite values. No bound on the sum of `frozen_indicator` on one device may be relied on, other than what follows from the above.
Results may differ from a plain program's by a relative error of at most 0.00002.
Values sent between devices are 32-bit elements; how exact they have to be, the bound alone decides.
No kernel may reach another device: no remote copies, remote signals or barrier semaphores. Data moves between devices by JAX's collectives and lax.ppermute only.
A program may use at most 64 MiB of HBM per device.

v0:
```python
import functools

import jax
import jax.numpy as jnp
from jax import lax
from jax.experimental import pallas as pl
from jax.experimental.pallas import tpu as pltpu
from jax.sharding import PartitionSpec as P

SUBS = 2
EVP = 20
LEVELS = 8
ROWS = 8
LANES = 128
SOURCES = 128
ICE_ROWS = 16
FIELDS = 3 * LEVELS
UP_ROWS = (2, 2, 1)
DOWN_ROWS = (2, 1, 1)
UP = LEVELS * sum(UP_ROWS)
DOWN = LEVELS * sum(DOWN_ROWS)
TILES = 32
STAGED = ("press", "zonal", "merid", "motion", "strain", "resist", "frozen")
AFTER = ("link", "site", "area", "heat", "target", "skin")

isentropic_lapse = 0.3
gravity_step = 0.5
floe_warmth = 2.0
floor_conductance = 1.0
relaxation = 0.5
stress_decay = 0.05
mobility = 0.3
water_drag = 0.1

BOTH = ("face", "tile")
VMEM = pl.BlockSpec(memory_space=pltpu.VMEM)


def struct(*shape):
    return jax.ShapeDtypeStruct(shape, jnp.float32)


def kept(*shape):
    return pltpu.VMEM(shape, jnp.float32)


def near(values):
    return pltpu.with_memory_space_constraint(values, pltpu.VMEM)


def lanes_of(shape):
    return lax.broadcasted_iota(jnp.int32, shape, len(shape) - 1)


def rows_of(shape):
    return lax.broadcasted_iota(jnp.int32, shape, len(shape) - 2)


def copies_of(sources, targets, sems):
    copies = [
        pltpu.make_async_copy(source, target, sems.at[at])
        for at, (source, target) in enumerate(zip(sources, targets))
    ]
    for copy in copies:
        copy.start()
    return copies


def slab_rows(counts, field, level):
    return pl.ds(LEVELS * sum(counts[:field]) + counts[field] * level, counts[field])


def stage_kernel(*refs):
    count = len(STAGED)
    targets = refs[count : 2 * count]
    side_out, down_out, up_out, sems = refs[2 * count :]
    copies = copies_of(refs[:count], targets, sems)
    motion_ref, strain_ref, resist_ref, frozen_ref = targets[3:7]
    for copy in copies[:3]:
        copy.wait()
    lane = lanes_of((ROWS, LANES))
    packed = jnp.zeros((ROWS, LANES), jnp.float32)
    for field, ref in enumerate(targets[:3]):
        for level in range(LEVELS):
            cells = ref[level]
            at = 4 * (field * LEVELS + level)
            moved = pltpu.roll(cells, 2 + at, 1)
            packed = jnp.where((lane >= at) & (lane < at + 4), moved, packed)
            down_out[slab_rows(DOWN_ROWS, field, level), :] = cells[: DOWN_ROWS[field]]
            up_out[slab_rows(UP_ROWS, field, level), :] = cells[ROWS - UP_ROWS[field] :]
    for copy in copies[3:]:
        copy.wait()
    edge = jnp.zeros((1, LANES), jnp.float32)
    lane = lanes_of((1, LANES))
    for row, first, shift in ((ICE_ROWS - 1, 0, EVP), (0, 3, 0)):
        here = pl.ds(row, 1)
        strength = resist_ref[here] * (0.1 + 0.9 * frozen_ref[here].astype(jnp.float32))
        for at, cells in enumerate((motion_ref[here], strain_ref[here], strength), first):
            moved = pltpu.roll(cells, (EVP * at + shift) % LANES, 1)
            edge = jnp.where((lane >= EVP * at) & (lane < EVP * at + EVP), moved, edge)
    edge = jnp.broadcast_to(edge, (ROWS, LANES))
    side_out[pl.ds(0, ROWS), :] = packed
    side_out[pl.ds(ROWS, ROWS), :] = edge
    down_out[pl.ds(DOWN, 2), :] = packed[:2]
    up_out[pl.ds(UP, 2), :] = packed[ROWS - 2 :]
    down_out[pl.ds(DOWN + 2, 6), :] = edge[:6]
    up_out[pl.ds(UP + 2, 6), :] = edge[:6]


def factor_kernel(*refs):
    count = len(AFTER)
    speed_ref, _, *refs = refs
    targets = refs[count : 2 * count]
    speed_out, gain_out, inverse_out, answer_out, slot_out, speeds, sems = refs[2 * count :]
    speed_copy = pltpu.make_async_copy(speed_ref, speeds, sems.at[count])
    speed_copy.start()
    copies = copies_of(refs[:count], targets, sems)
    link_ref, site_ref, area_ref = targets[:3]
    copies[0].wait()
    link = link_ref[0]
    inverse = 1.0 / (1.0 + link)
    gain = link * inverse
    inverse_out[0] = inverse
    gain_out[0] = gain
    for level in range(1, LEVELS - 1):
        earlier, link = link, link_ref[level]
        inverse = 1.0 / (1.0 + earlier + link - earlier * gain)
        gain = link * inverse
        inverse_out[level] = inverse
        gain_out[level] = gain
    inverse = 1.0 / (1.0 + link * (1.0 - gain))
    beta = gravity_step * inverse
    inverse_out[LEVELS - 1] = inverse
    answer_out[LEVELS - 1] = answer = beta
    for level in range(LEVELS - 2, -1, -1):
        answer = gain_out[level] * answer
        answer_out[level] = answer
    drag = link_ref[LEVELS - 1]
    table = spread_rows(drag / (1.0 + drag * beta))
    for copy in copies[1:3]:
        copy.wait()
    for start in range(0, SOURCES, ROWS):
        here = pl.ds(start, ROWS)
        (found,) = look_up((table,), site_ref[here, :])
        slot_out[here, :] = area_ref[here, :] * found
    speed_copy.wait()
    for level in range(LEVELS):
        speed_out[pl.ds(level, 1), :] = jnp.full((1, LANES), speeds[level])
    for copy in copies[3:]:
        copy.wait()


def side_kernel(side_ref, above_ref, below_ref, out_ref):
    out_ref[pl.ds(0, ROWS + 3), :] = side_ref[pl.ds(0, ROWS + 3), :]
    out_ref[pl.ds(8, 2), :] = above_ref[pl.ds(DOWN, 2), :]
    out_ref[pl.ds(11, 1), :] = below_ref[pl.ds(UP + 2, 1), :]
    out_ref[pl.ds(12, 2), :] = above_ref[pl.ds(DOWN + 2, 2), :]
    out_ref[pl.ds(14, 2), :] = below_ref[pl.ds(UP, 2), :]


def widen_kernel(p_ref, u_ref, v_ref, above_ref, below_ref, wide_out):
    for field, ref in enumerate((p_ref, u_ref, v_ref)):
        above, below = DOWN_ROWS[field], UP_ROWS[field]
        for level in range(LEVELS):
            at = field * LEVELS + level
            wide_out[at, pl.ds(0, ROWS), :] = ref[level]
            wide_out[at, pl.ds(8, 8), :] = jnp.zeros((8, LANES), jnp.float32)
            wide_out[at, pl.ds(8, above), :] = above_ref[slab_rows(DOWN_ROWS, field, level), :]
            wide_out[at, pl.ds(16 - below, below), :] = below_ref[
                slab_rows(UP_ROWS, field, level), :
            ]


def look_up(tables, index):
    high = index // LANES
    low = index % LANES
    found = [None] * len(tables)
    for row in range(len(tables[0])):
        here = high == row
        for at, rows in enumerate(tables):
            taken = jnp.take_along_axis(rows[row], low, axis=1, mode="promise_in_bounds")
            found[at] = taken if row == 0 else jnp.where(here, taken, found[at])
    return found


def spread_rows(table):
    return [
        jnp.broadcast_to(table[row : row + 1], (ROWS, LANES)) for row in range(table.shape[0])
    ]


def columns_kernel(
    speed_ref,
    wide_ref,
    heat_ref,
    link_ref,
    site_ref,
    area_ref,
    inverse_ref,
    weight_ref,
    twin_ref,
    cross_ref,
    press_out,
    rest_out,
    halo_out,
    slots_out,
):
    shape = (2 * ROWS, LANES)
    place = lax.axis_index("tile")
    even = place % 2 == 0
    left = jnp.where(even, cross_ref[...], twin_ref[...])
    right = jnp.where(even, twin_ref[...], cross_ref[...])
    border = jnp.where(lanes_of(shape) % 4 < 2, left, right)
    temps = []
    for level in range(LEVELS):
        speed = jnp.broadcast_to(speed_ref[pl.ds(level, 1), 0:1], (2 * ROWS, 2 * LANES))
        now = []
        for field in range(3):
            at = field * LEVELS + level
            outer = pltpu.roll(border, (126 - 4 * at) % LANES, 1)
            now.append(jnp.concatenate([wide_ref[at], outer], axis=1))
        press, zonal, merid = now
        for _ in range(SUBS):
            zonal = zonal - speed * (pltpu.roll(press, 15, 0) - press)
            merid = merid - speed * (pltpu.roll(press, 255, 1) - press)
            press = press - speed * (
                zonal - pltpu.roll(zonal, 1, 0) + merid - pltpu.roll(merid, 1, 1)
            )
        final = press[:ROWS, :LANES]
        press_out[level] = final
        temps.append(heat_ref[level] + isentropic_lapse * final)
    last_zonal = zonal[:ROWS, :LANES]
    last_merid = merid[:ROWS, :LANES]

    rest = temps[0] * inverse_ref[0]
    rest_out[0] = rest
    for level in range(1, LEVELS):
        rest = (temps[level] + link_ref[level - 1] * rest) * inverse_ref[level]
        rest_out[level] = rest
    gamma = rest
    stress = link_ref[LEVELS - 1] * (last_zonal + 0.5 * last_merid)

    tables = [spread_rows(table) for table in (gamma, stress)]
    for start in range(0, SOURCES, ROWS):
        here = pl.ds(start, ROWS)
        found = look_up(tables, site_ref[here, :])
        slot_w = weight_ref[here, :]
        slots_out[pl.ds(3 * start, ROWS, stride=3), :] = slot_w
        slots_out[pl.ds(3 * start + 1, ROWS, stride=3), :] = slot_w * found[0]
        slots_out[pl.ds(3 * start + 2, ROWS, stride=3), :] = area_ref[here, :] * found[1]
    before = jnp.where(place == 0, left[11:12], left[10:11])
    after = jnp.where(place == TILES - 1, right[12:13], right[10:11])
    for at in range(3):
        halo_out[pl.ds(at, 1), :] = pltpu.roll(before, LANES - EVP - EVP * at, 1)
        halo_out[pl.ds(4 + at, 1), :] = pltpu.roll(after, LANES - EVP * (at + 3), 1)


def in_three(values):
    first = values.astype(jnp.bfloat16)
    left = values - first.astype(jnp.float32)
    second = left.astype(jnp.bfloat16)
    third = (left - second.astype(jnp.float32)).astype(jnp.bfloat16)
    return first.astype(jnp.float32), second.astype(jnp.float32), third.astype(jnp.float32)


def segment_sums(read, index_ref, values, high_row, low_count, group=32):
    high_count = len(high_row)
    shape = (high_count, LANES)
    rows = rows_of(shape)
    high_here = sum(jnp.where(rows == at, high, 0) for high, at in enumerate(high_row))
    low_here = rows_of((low_count, LANES))
    count = 3 * values * high_count

    def step(block, total):
        start = pl.multiple_of(block * group, group)
        index = index_ref[pl.ds(start, group), :]
        high = index // low_count
        low = index % low_count
        parts = [part for value in range(values) for part in in_three(read(value, start, group))]
        carried, spread = [], []
        for row in range(group):
            here = high_here == high[row : row + 1]
            carried.append(
                jnp.concatenate(
                    [
                        jnp.where(here, jnp.broadcast_to(part[row : row + 1], shape), 0.0).astype(
                            jnp.bfloat16
                        )
                        for part in parts
                    ],
                    axis=0,
                )
            )
            spread.append(
                jnp.where(low_here == low[row : row + 1], 1.0, 0.0).astype(jnp.bfloat16)
            )
        return total + lax.dot_general(
            jnp.concatenate(carried, axis=1),
            jnp.concatenate(spread, axis=1),
            (((1,), (1,)), ((), ())),
            preferred_element_type=jnp.float32,
        )

    total = lax.fori_loop(
        0, SOURCES // group, step, jnp.zeros((count, low_count), jnp.float32), unroll=True
    )
    sums = []
    for value in range(values):
        at = 3 * value * high_count
        sums.append(
            total[at + 2 * high_count : at + 3 * high_count]
            + total[at + high_count : at + 2 * high_count]
            + total[at : at + high_count]
        )
    return sums


def ice_kernel(
    slots_ref, target_ref, skin_ref, frozen_ref, resist_ref, _, skin_out, flux_out, ice_out
):
    def read(value, start, group):
        return slots_ref[pl.ds(3 * start + value, group, stride=3), :]

    heat, warmth, tau = segment_sums(read, target_ref, 3, range(ICE_ROWS), LANES, group=8)
    skin = skin_ref[...]
    frozen = frozen_ref[...]
    fresh = jnp.where(
        frozen == 1,
        (floe_warmth * skin + warmth) / (floe_warmth + floor_conductance + heat),
        skin,
    )
    skin_out[...] = fresh
    table = spread_rows(fresh)
    for start in range(0, SOURCES, ROWS):
        (at_floe,) = look_up((table,), target_ref[pl.ds(start, ROWS), :])
        flux_out[pl.ds(2 * start, ROWS, stride=2), :] = (
            slots_ref[pl.ds(3 * start, ROWS, stride=3), :] * at_floe
            - slots_ref[pl.ds(3 * start + 1, ROWS, stride=3), :]
        )
    ends = jnp.where(
        lanes_of((1, LANES)) < LANES // 2, tau[0:1], tau[ICE_ROWS - 1 : ICE_ROWS]
    )
    flux_out[pl.ds(1, SOURCES, stride=2), :] = jnp.broadcast_to(ends, (SOURCES, LANES))
    ice_out[0] = resist_ref[...] * (0.1 + 0.9 * frozen.astype(jnp.float32))
    ice_out[1] = tau


def paired(even_rows, odd_rows):
    lane = lanes_of((ROWS, LANES))
    out = []
    for at in range(2):
        index = (2 * lane + at) % LANES
        out.append(
            jnp.where(
                lane < LANES // 2,
                jnp.take_along_axis(even_rows, index, axis=1, mode="promise_in_bounds"),
                jnp.take_along_axis(odd_rows, index, axis=1, mode="promise_in_bounds"),
            )
        )
    return out


def neighbourhood(even_rows, odd_rows, before, after):
    shape = (ROWS, LANES)
    lane = lanes_of(shape)
    row = rows_of(shape)
    own = paired(even_rows, odd_rows)
    behind = paired(jnp.broadcast_to(before, shape), jnp.broadcast_to(before, shape))
    ahead = paired(jnp.broadcast_to(after, shape), jnp.broadcast_to(after, shape))
    cells = {}
    for at in range(2):
        cells[at] = own[at]
        up = jnp.where(row == ROWS - 1, ahead[at], pltpu.roll(own[at], ROWS - 1, 0))
        down = jnp.where(row == 0, behind[at], pltpu.roll(own[at], 1, 0))
        for far in range(1, EVP // 2 + 1):
            cells[at + 2 * far] = pltpu.roll(
                jnp.where(lane < far, up, own[at]), LANES - far, 1
            )
            cells[at - 2 * far] = pltpu.roll(
                jnp.where(lane >= LANES - far, down, own[at]), far, 1
            )
    return cells


def drift_kernel(motion_ref, strain_ref, ice_ref, halo_ref, out_ref, held):
    place = lax.axis_index("face") * TILES + lax.axis_index("tile")
    blank = jnp.zeros((1, LANES), jnp.float32)
    even, odd = pl.ds(0, ROWS, stride=2), pl.ds(1, ROWS, stride=2)
    first = jnp.where(place == 0, 0.0, 1.0)
    last = jnp.where(place == SOURCES - 1, 0.0, 1.0)
    slow = 1.0 / (1.0 + mobility * water_drag)
    fade = 1.0 / (1.0 + stress_decay)
    arrays = (
        (motion_ref[even], motion_ref[odd], halo_ref[0:1], halo_ref[4:5], 1.0),
        (strain_ref[even], strain_ref[odd], halo_ref[1:2], halo_ref[5:6], mobility * slow),
        (
            ice_ref[0, even],
            ice_ref[0, odd],
            halo_ref[2:3],
            halo_ref[6:7],
            mobility * slow * relaxation * fade,
        ),
        (ice_ref[1, even], ice_ref[1, odd], blank, blank, mobility * slow),
    )
    for at, (even_rows, odd_rows, before, after, scale) in enumerate(arrays):
        cells = neighbourhood(
            even_rows * scale,
            odd_rows * scale,
            before * (first * scale),
            after * (last * scale),
        )
        for cell, values in cells.items():
            held[at, cell + EVP] = values
    shape = (ROWS, LANES)
    where = LANES * rows_of(shape) + lanes_of(shape)

    def inside(cell):
        end = (ROWS * LANES * 2 - cell) // 2
        return jnp.where((where == end) & (place == SOURCES - 1), 0.0, 1.0)

    width = 2 * EVP + 2
    velocity = [held[0, at] for at in range(width)]
    stress = [held[1, at] for at in range(width)]
    for turn in range(EVP):
        for at in range(turn, width - turn - 1):
            stress[at] = stress[at] * fade + held[2, at] * (velocity[at + 1] - velocity[at])
        for at in range(turn + 1, width - turn - 1):
            force = stress[at] - stress[at - 1] + held[3, at]
            if at >= EVP + 2 and at % 2 == 0:
                force = force * inside(at - EVP)
            velocity[at] = velocity[at] * slow + force
    lane = lanes_of(shape)
    for rows, half in ((even, 0), (odd, LANES // 2)):
        index = lane // 2 + half
        out_ref[rows] = jnp.where(
            lane % 2 == 0,
            jnp.take_along_axis(velocity[EVP], index, axis=1, mode="promise_in_bounds"),
            jnp.take_along_axis(velocity[EVP + 1], index, axis=1, mode="promise_in_bounds"),
        )


def edge_kernel(
    resist_ref, frozen_ref, halo_ref, gain_ref, rest_ref, out_ref, calm_out, held
):
    calm_out[LEVELS - 1] = calm = rest_ref[LEVELS - 1]
    for level in range(LEVELS - 2, -1, -1):
        calm = gain_ref[level] * calm + rest_ref[level]
        calm_out[level] = calm
    slow = 1.0 / (1.0 + mobility * water_drag)
    fade = 1.0 / (1.0 + stress_decay)
    half = LANES // 2
    here = lanes_of((1, LANES)) < half
    ends = [
        resist_ref[pl.ds(row, 1)] * (0.1 + 0.9 * frozen_ref[pl.ds(row, 1)].astype(jnp.float32))
        for row in (0, ICE_ROWS - 1)
    ]
    strength = (
        jnp.where(here, ends[0], halo_ref[2:3]),
        jnp.where(here, halo_ref[6:7], ends[1]),
    )
    pull = jnp.concatenate(
        [jnp.broadcast_to(pltpu.roll(row, half, 1), (24, LANES)) for row in strength], axis=0
    ) * (mobility * slow * relaxation * fade)
    shape = (48, LANES)
    row = rows_of(shape)
    lane = lanes_of(shape)
    source = jnp.where(row < 24, half - EVP + row, half - 24 + row)
    push = jnp.where((lane == source) & (row % 24 < EVP), mobility * slow, 0.0)
    velocity = jnp.zeros(shape, jnp.float32)
    stress = jnp.zeros(shape, jnp.float32)
    for _ in range(EVP):
        stress = stress * fade + pull * (pltpu.roll(velocity, LANES - 1, 1) - velocity)
        velocity = velocity * slow + (stress - pltpu.roll(stress, 1, 1) + push)
    velocity = pltpu.roll(velocity, half, 1)
    velocity = jnp.where(
        ((row < 24) & (lane < EVP)) | ((row >= 24) & (lane >= LANES - EVP)), velocity, 0.0
    )
    held[...] = jnp.zeros((LANES, LANES), jnp.float32)
    held[pl.ds(0, EVP), :] = velocity[24 : 24 + EVP]
    held[pl.ds(LANES - EVP, EVP), :] = velocity[:EVP]
    out_ref[...] = jnp.concatenate(in_three(held[...]), axis=1).astype(jnp.bfloat16)


def last_kernel(
    flux_ref, site_ref, answer_ref, calm_ref, drift_ref, edge_ref, heat_out, motion_out
):
    def read(value, start, group):
        return flux_ref[pl.ds(2 * start, group, stride=2), :]

    place = lax.axis_index("face") * TILES + lax.axis_index("tile")
    lane = lanes_of((1, LANES))
    before = flux_ref[pl.ds(2 * jnp.maximum(place - 1, 0) + 1, 1), :]
    after = flux_ref[pl.ds(2 * jnp.minimum(place + 1, SOURCES - 1) + 1, 1), :]
    outside = jnp.where(
        lane < LANES // 2,
        after * jnp.where(place == SOURCES - 1, 0.0, 1.0),
        before * jnp.where(place == 0, 0.0, 1.0),
    )
    products = lax.dot_general(
        jnp.concatenate(
            [jnp.broadcast_to(part, (ROWS, LANES)) for part in in_three(outside)]
            + [jnp.zeros((ROWS, LANES), jnp.float32)],
            axis=0,
        ).astype(jnp.bfloat16),
        edge_ref[...],
        (((1,), (0,)), ((), ())),
        preferred_element_type=jnp.float32,
    )
    by_part = [
        products[:, LANES * part : LANES * (part + 1)] for part in range(3)
    ]
    by_part = [part[:ROWS] + part[ROWS : 2 * ROWS] + part[2 * ROWS : 3 * ROWS] for part in by_part]
    added = (by_part[0] + by_part[1] + by_part[2])[0:1]
    motion_out[...] = drift_ref[...]
    motion_out[0:1] = drift_ref[0:1] + jnp.where(lane < EVP, added, 0.0)
    end = pl.ds(ICE_ROWS - 1, 1)
    motion_out[end] = drift_ref[end] + jnp.where(lane >= LANES - EVP, added, 0.0)

    order = [ROWS * (half % 2) + half // 2 for half in range(2 * ROWS)]
    (halves,) = segment_sums(read, site_ref, 1, order, LANES // 2)
    surface_flux = jnp.concatenate([halves[:ROWS], halves[ROWS:]], axis=1)
    for level in range(LEVELS):
        heat_out[level] = answer_ref[level] * surface_flux + calm_ref[level]


def ring(axis, step):
    count = lax.axis_size(axis)
    return [(i, (i + step) % count) for i in range(count)]


def swaps(axis, first):
    count = lax.axis_size(axis)
    pairs = [(i, (i + 1) % count) for i in range(first, count, 2)]
    return sorted(pairs + [(b, a) for a, b in pairs])


def exchanged(rows, count):
    blocks = rows.reshape(SOURCES, count, 1, LANES)
    blocks = lax.all_to_all(blocks, BOTH, split_axis=0, concat_axis=0, tiled=True)
    return near(blocks.reshape(SOURCES * count, LANES))


def local(
    squeeze_anomaly,
    eastward_airflow,
    northward_airflow,
    thermal_anomaly,
    diffusivity_link,
    sound_stability_ratio,
    overlay_source_site,
    overlay_target_floe,
    overlay_fraction,
    floe_skin_kelvin,
    frozen_indicator,
    floe_motion,
    floe_strain_tensor,
    floe_compress_resist,
):
    ice = (ICE_ROWS, LANES)
    slot = (SOURCES, LANES)
    arguments = dict(
        press=squeeze_anomaly,
        zonal=eastward_airflow,
        merid=northward_airflow,
        motion=floe_motion.reshape(ice),
        strain=floe_strain_tensor.reshape(ice),
        resist=floe_compress_resist.reshape(ice),
        frozen=frozen_indicator.reshape(ice),
        skin=floe_skin_kelvin.reshape(ice),
        heat=thermal_anomaly,
        link=diffusivity_link,
        site=overlay_source_site.reshape(slot),
        area=overlay_fraction.reshape(slot),
        target=overlay_target_floe.reshape(slot),
    )
    hbm = pl.BlockSpec(memory_space=pl.ANY)
    sources = [arguments[name] for name in STAGED]
    *staged, sides, down, up = pl.pallas_call(
        stage_kernel,
        out_shape=[pltpu.VMEM(source.shape, source.dtype) for source in sources]
        + [kept(2 * ROWS, LANES), kept(DOWN + 8, LANES), kept(UP + 8, LANES)],
        in_specs=[hbm] * len(sources),
        out_specs=[VMEM] * (len(sources) + 3),
        scratch_shapes=[pltpu.SemaphoreType.DMA((len(sources),))],
    )(*sources)
    at = {name: near(values) for name, values in zip(STAGED, staged)}
    sides = near(sides)
    sources = [arguments[name] for name in AFTER]
    *staged, speeds, gain, inverse, answer, weight = pl.pallas_call(
        factor_kernel,
        out_shape=[pltpu.VMEM(source.shape, source.dtype) for source in sources]
        + [kept(LEVELS, LANES)]
        + [kept(LEVELS, ROWS, LANES)] * 3
        + [kept(*slot)],
        in_specs=[hbm, VMEM] + [hbm] * len(sources),
        out_specs=[VMEM] * (len(sources) + 5),
        scratch_shapes=[
            pltpu.SMEM((LEVELS,), jnp.float32),
            pltpu.SemaphoreType.DMA((len(sources) + 1,)),
        ],
    )(sound_stability_ratio, sides, *sources)
    at.update({name: near(values) for name, values in zip(AFTER, staged)})
    above = near(lax.ppermute(down, "face", ring("face", -1)))
    below = near(lax.ppermute(up, "face", ring("face", 1)))
    sides = pl.pallas_call(
        side_kernel, out_shape=kept(2 * ROWS, LANES), in_specs=[VMEM] * 3, out_specs=VMEM
    )(sides, above, below)
    wide = pl.pallas_call(
        widen_kernel, out_shape=kept(FIELDS, 2 * ROWS, LANES), in_specs=[VMEM] * 5, out_specs=VMEM
    )(*(at[name] for name in ("press", "zonal", "merid")), above, below)
    twin = near(lax.ppermute(sides, "tile", swaps("tile", 0)))
    cross = near(lax.ppermute(sides, "tile", swaps("tile", 1)))
    pressure_new, rest, halo, slots = pl.pallas_call(
        columns_kernel,
        out_shape=[
            struct(LEVELS, ROWS, LANES),
            kept(LEVELS, ROWS, LANES),
            kept(8, LANES),
            struct(3 * SOURCES, LANES),
        ],
        in_specs=[VMEM] * 10,
        out_specs=[VMEM] * 4,
    )(
        near(speeds),
        near(wide),
        at["heat"],
        at["link"],
        at["site"],
        at["area"],
        near(inverse),
        near(weight),
        twin,
        cross,
    )
    arrived = exchanged(slots, 3)
    edge, calm = pl.pallas_call(
        edge_kernel,
        out_shape=[pltpu.VMEM((LANES, 3 * LANES), jnp.bfloat16), kept(LEVELS, ROWS, LANES)],
        in_specs=[VMEM] * 5,
        out_specs=[VMEM] * 2,
        scratch_shapes=[pltpu.VMEM((LANES, LANES), jnp.float32)],
    )(at["resist"], at["frozen"], near(halo), near(gain), near(rest))
    edge = near(edge)
    fresh, flux, ice_terms = pl.pallas_call(
        ice_kernel,
        out_shape=[struct(*ice), struct(2 * SOURCES, LANES), kept(2, *ice)],
        in_specs=[VMEM] * 6,
        out_specs=[VMEM] * 3,
    )(arrived, *(at[name] for name in ("target", "skin", "frozen", "resist")), edge)
    returned = exchanged(flux, 2)
    drifted = pl.pallas_call(
        drift_kernel,
        out_shape=kept(*ice),
        in_specs=[VMEM] * 4,
        out_specs=VMEM,
        scratch_shapes=[pltpu.VMEM((4, 2 * EVP + 2, ROWS, LANES), jnp.float32)],
    )(at["motion"], at["strain"], near(ice_terms), near(halo))
    temp_new, velocity = pl.pallas_call(
        last_kernel,
        out_shape=[struct(LEVELS, ROWS, LANES), struct(*ice)],
        in_specs=[VMEM] * 6,
        out_specs=[VMEM] * 2,
    )(returned, at["site"], near(answer), near(calm), near(drifted), edge)
    return (temp_new, pressure_new, fresh.reshape(-1), velocity.reshape(-1))


def solution(mesh):
    block = P(None, "face", "tile")
    slot = P(BOTH, None, None)
    cells = P(BOTH)
    return jax.shard_map(
        local,
        mesh=mesh,
        in_specs=(block,) * 5 + (P(),) + (slot,) * 3 + (cells,) * 5,
        out_specs=(block, block, cells, cells),
        check_vma=False,
    )
```

profile of v0, /device:TPU:1, one launch (start us, length us, event | category | flops | bytes accessed | tf_op | source)
XLA Modules:
  0.0 53.2 jit_solution(8506730009372717081)
XLA Ops:
  0.6 1.0 %shard_map.165 = (f32[8,8,128]{2,1,0:T(8,128)S(1)}, f32[8,8,128]{2,1,0:T(8,128)S(1)}, f32[8,8,128]{2,1,0:T(8,128)S(1)}, f32[16,128]{1,0:T(8,128)S(1)}, f32[16,12...) custom-call(f32[8,8,128]{2,1,0:T(8,128)} %refs_0_.2, ...), custom_call_target="tpu_custom_call" | custom-call | tf_op jit(solution)/shard_map/pallas_call | solution.py:578
  1.7 2.1 %collective-permute-start.1 = (f32[48,128]{1,0:T(8,128)S(1)}, f32[48,128]{1,0:T(8,128)S(1)}, u32[]{:S(2)}, u32[]{:S(2)}) collective-permute-start(f32[48,128]{1,0:T(8,128)S(1)} %get-tuple-element.42), channel_id=1, source_target_pairs={{0,32},{32,64},{64,96},{96,0},{1,33},{33,65},{65,97},{97,1},{2,34}... | collective-permute-start | bytes 73736 | tf_op jit(solution)/shard_map/ppermute | solution.py:604
  3.8 1.3 %collective-permute-start = (f32[40,128]{1,0:T(8,128)S(1)}, f32[40,128]{1,0:T(8,128)S(1)}, u32[]{:S(2)}, u32[]{:S(2)}) collective-permute-start(f32[40,128]{1,0:T(8,128)S(1)} %get-tuple-element.41), channel_id=1, source_target_pairs={{0,96},{32,0},{64,32},{96,64},{1,97},{33,1},{65,33},{97,65},{2,98}... | collective-permute-start | bytes 61448 | tf_op jit(solution)/shard_map/ppermute | solution.py:603
  5.1 1.3 %collective-permute-done.above_ref = f32[40,128]{1,0:T(8,128)S(1)} collective-permute-done((f32[40,128]{1,0:T(8,128)S(1)}, f32[40,128]{1,0:T(8,128)S(1)}, u32[]{:S(2)}, u32[]{:S(2)}) %collective-permute-start) | collective-permute-done | bytes 20512 | tf_op jit(solution)/shard_map/ppermute | solution.py:603
  6.4 0.0 collective-permute-done.1.below_ref
  6.4 3.3 %collective-permute-start.3 = (f32[16,128]{1,0:T(8,128)S(1)}, f32[16,128]{1,0:T(8,128)S(1)}, u32[]{:S(2)}, u32[]{:S(2)}) collective-permute-start(f32[16,128]{1,0:T(8,128)S(1)} %shard_map.168), channel_id=1, source_target_pairs={{0,31},{1,2},{2,1},{3,4},{4,3},{5,6},{6,5},{7,8},{8,7},{9,10},{10,... | collective-permute-start | bytes 24584 | tf_op jit(solution)/shard_map/ppermute | solution.py:612
  9.7 3.4 %collective-permute-start.2 = (f32[16,128]{1,0:T(8,128)S(1)}, f32[16,128]{1,0:T(8,128)S(1)}, u32[]{:S(2)}, u32[]{:S(2)}) collective-permute-start(f32[16,128]{1,0:T(8,128)S(1)} %shard_map.168), channel_id=1, source_target_pairs={{0,1},{1,0},{2,3},{3,2},{4,5},{5,4},{6,7},{7,6},{8,9},{9,8},{10,11... | collective-permute-start | bytes 24584 | tf_op jit(solution)/shard_map/ppermute | solution.py:611
  13.1 1.2 %shard_map.166 = (f32[8,8,128]{2,1,0:T(8,128)S(1)}, s32[128,128]{1,0:T(8,128)S(1)}, f32[128,128]{1,0:T(8,128)S(1)}, f32[8,8,128]{2,1,0:T(8,128)S(1)}, s32[128,12...) custom-call(f32[8]{0:T(128)} %refs_0_.3, ...), custom_call_target="tpu_custom_call" | custom-call | tf_op jit(solution)/shard_map/pallas_call | solution.py:589
  14.4 0.0 collective-permute-done.3.cross_ref
  14.4 0.0 collective-permute-done.2.twin_ref
  14.4 1.5 %shard_map.169 = (f32[8,8,128]{2,1,0:T(8,128)}, f32[8,8,128]{2,1,0:T(8,128)S(1)}, f32[8,128]{1,0:T(8,128)S(1)}, f32[384,128]{1,0:T(8,128)}) custom-call(f32[8,128]{1,0:T(8,128)S(1)} %get-tuple-element.37.speed_ref, f32[24,16,128]{2,1,0:T(8,128)S(1)} %shard_map.167.wide_ref, f32[8,8,128]{2,1,0:T(8,128)S(1)} %get-tuple-element.43.heat_ref, ...), custom_call_target="tpu_custom_call" | custom-call | tf_op jit(solution)/shard_map/pallas_call | solution.py:613
  15.8 8.4 %all-to-all-start = ((f32[128,3,1,128]{3,2,1,0:T(1,128)}), f32[128,3,1,128]{3,2,1,0:T(1,128)S(1)}, u32[]{:S(2)}, u32[]{:S(2)}) async-start(f32[128,3,1,128]{3,2,1,0:T(1,128)} %bitcast.18), calls=%async_computation | async-start | bytes 393216 | tf_op jit(solution)/shard_map/all_to_all | solution.py:539
  24.2 2.9 %shard_map.170 = (bf16[128,384]{1,0:T(8,128)(2,1)S(1)}, f32[8,8,128]{2,1,0:T(8,128)S(1)}) custom-call(f32[16,128]{1,0:T(8,128)S(1)} %get-tuple-element.53.resist_ref, s32[16,128]{1,0:T(8,128)S(1)} %get-tuple-element.52.frozen_ref, f32[8,128]{1,0:T(8,128)S(1)} %get-tuple-element.54.halo_ref, f32[8,8,128]{2,1,0:T(8,128)S(1)} %get-tuple-element.55.gain_ref, ...), custom_call_target="tpu_custom_call" | custom-call | tf_op jit(solution)/shard_map/pallas_call | solution.py:636
  27.1 7.5 %all-to-all-done = f32[128,3,1,128]{3,2,1,0:T(1,128)S(1)} async-done(((f32[128,3,1,128]{3,2,1,0:T(1,128)}), f32[128,3,1,128]{3,2,1,0:T(1,128)S(1)}, u32[]{:S(2)}, u32[]{:S(2)}) %all-to-all-start) | async-done | bytes 196640 | tf_op jit(solution)/shard_map/all_to_all | solution.py:539
  34.6 2.7 %shard_map.171 = (f32[16,128]{1,0:T(8,128)}, f32[256,128]{1,0:T(8,128)}, f32[2,16,128]{2,1,0:T(8,128)S(1)}) custom-call(f32[384,128]{1,0:T(8,128)S(1)} %bitcast.16, s32[128,128]{1,0:T(8,128)S(1)} %get-tuple-element.50.target_ref, f32[16,128]{1,0:T(8,128)S(1)} %get-tuple-element.51.skin_ref, s32[16,128]{1,0:T(8,128)S(1)} %get-tuple-element.52.frozen_ref, ...), custom_call_target="tpu_custom_call" | custom-call | tf_op jit(solution)/shard_map/pallas_call | solution.py:644
  37.2 4.5 %all-to-all-start.1 = ((f32[128,2,1,128]{3,1,2,0:T(2,128)}), f32[128,2,1,128]{3,1,2,0:T(2,128)S(1)}, u32[]{:S(2)}, u32[]{:S(2)}) async-start(f32[128,2,1,128]{3,1,2,0:T(2,128)} %bitcast.19), calls=%async_computation.1 | async-start | bytes 262144 | tf_op jit(solution)/shard_map/all_to_all | solution.py:539
  41.7 0.8 %shard_map.172.drift_ref = f32[16,128]{1,0:T(8,128)S(1)} custom-call(f32[16,128]{1,0:T(8,128)S(1)} %get-tuple-element.61.motion_ref, f32[16,128]{1,0:T(8,128)S(1)} %get-tuple-element.62.strain_ref, f32[2,16,128]{2,1,0:T(8,128)S(1)} %get-tuple-element.63.ice_ref, f32[8,128]{1,0:T(8,128)S(1)} %get-tuple-element.54.halo_ref), custom_call_target="tpu_custom_call" | custom-call | tf_op jit(solution)/shard_map/pallas_call | solution.py:651
  42.5 9.2 %all-to-all-done.1 = f32[128,2,1,128]{3,1,2,0:T(2,128)S(1)} async-done(((f32[128,2,1,128]{3,1,2,0:T(2,128)}), f32[128,2,1,128]{3,1,2,0:T(2,128)S(1)}, u32[]{:S(2)}, u32[]{:S(2)}) %all-to-all-start.1) | async-done | bytes 131104 | tf_op jit(solution)/shard_map/all_to_all | solution.py:539
  51.7 1.6 %shard_map.173 = (f32[8,8,128]{2,1,0:T(8,128)}, f32[16,128]{1,0:T(8,128)}) custom-call(f32[256,128]{1,0:T(8,128)S(1)} %bitcast.17, s32[128,128]{1,0:T(8,128)S(1)} %get-tuple-element.45.site_ref, f32[8,8,128]{2,1,0:T(8,128)S(1)} %get-tuple-element.59.answer_ref, f32[8,8,128]{2,1,0:T(8,128)S(1)} %get-tuple-element.60.calm_ref, ...), custom_call_target="tpu_custom_call" | custom-call | tf_op jit(solution)/shard_map/pallas_call | solution.py:658
  (2 shorter events, 0.0 us)
Async XLA Ops:
  1.7 4.7 %collective-permute-start.1 = (f32[48,128]{1,0:T(8,128)S(1)}, f32[48,128]{1,0:T(8,128)S(1)}, u32[]{:S(2)}, u32[]{:S(2)}) collective-permute-start(f32[48,128]{1,0:T(8,128)S(1)} %get-tuple-element.42), channel_id=1, source_target_pairs={{0,32},{32,64},{64,96},{96,0},{1,33},{33,65},{65,97},{97,1},{2,34}... | collective-permute-start | bytes 73736 | tf_op jit(solution)/shard_map/ppermute | solution.py:604
  3.8 2.6 %collective-permute-start = (f32[40,128]{1,0:T(8,128)S(1)}, f32[40,128]{1,0:T(8,128)S(1)}, u32[]{:S(2)}, u32[]{:S(2)}) collective-permute-start(f32[40,128]{1,0:T(8,128)S(1)} %get-tuple-element.41), channel_id=1, source_target_pairs={{0,96},{32,0},{64,32},{96,64},{1,97},{33,1},{65,33},{97,65},{2,98}... | collective-permute-start | bytes 61448 | tf_op jit(solution)/shard_map/ppermute | solution.py:603
  6.4 7.9 %collective-permute-start.3 = (f32[16,128]{1,0:T(8,128)S(1)}, f32[16,128]{1,0:T(8,128)S(1)}, u32[]{:S(2)}, u32[]{:S(2)}) collective-permute-start(f32[16,128]{1,0:T(8,128)S(1)} %shard_map.168), channel_id=1, source_target_pairs={{0,31},{1,2},{2,1},{3,4},{4,3},{5,6},{6,5},{7,8},{8,7},{9,10},{10,... | collective-permute-start | bytes 24584 | tf_op jit(solution)/shard_map/ppermute | solution.py:612
  9.7 4.6 %collective-permute-start.2 = (f32[16,128]{1,0:T(8,128)S(1)}, f32[16,128]{1,0:T(8,128)S(1)}, u32[]{:S(2)}, u32[]{:S(2)}) collective-permute-start(f32[16,128]{1,0:T(8,128)S(1)} %shard_map.168), channel_id=1, source_target_pairs={{0,1},{1,0},{2,3},{3,2},{4,5},{5,4},{6,7},{7,6},{8,9},{9,8},{10,11... | collective-permute-start | bytes 24584 | tf_op jit(solution)/shard_map/ppermute | solution.py:611
  15.8 18.8 %all-to-all-start = ((f32[128,3,1,128]{3,2,1,0:T(1,128)}), f32[128,3,1,128]{3,2,1,0:T(1,128)S(1)}, u32[]{:S(2)}, u32[]{:S(2)}) async-start(f32[128,3,1,128]{3,2,1,0:T(1,128)} %bitcast.18), calls=%async_computation | async-start | bytes 393216 | tf_op jit(solution)/shard_map/all_to_all | solution.py:539
  37.2 14.4 %all-to-all-start.1 = ((f32[128,2,1,128]{3,1,2,0:T(2,128)}), f32[128,2,1,128]{3,1,2,0:T(2,128)S(1)}, u32[]{:S(2)}, u32[]{:S(2)}) async-start(f32[128,2,1,128]{3,1,2,0:T(2,128)} %bitcast.19), calls=%async_computation.1 | async-start | bytes 262144 | tf_op jit(solution)/shard_map/all_to_all | solution.py:539
where the time goes:
time: 53.5 us; the launch traced here: 53.2 us
  starting transfers between devices  23 us (43%)
  waiting for transfers between devices  17.9 us (33%)
  Pallas kernels  11.7 us (22%)
  between operations  0.7 us (1%)
    all_to_all x2, waiting for transfers between devices, exchanged(): lax.all_to_all(blocks, BOTH, split_axis=0, concat_axis=0, tiled=True)  16.6 us
    all_to_all x2, starting transfers between devices, exchanged(): lax.all_to_all(blocks, BOTH, split_axis=0, concat_axis=0, tiled=True)  12.9 us
    ppermute x1, starting transfers between devices, local(): twin = near(lax.ppermute(sides, 'tile', swaps('tile', 0)))  3.35 us
    ppermute x1, starting transfers between devices, local(): cross = near(lax.ppermute(sides, 'tile', swaps('tile', 1)))  3.29 us
    pallas_call x1, Pallas kernels, local(): pl.pallas_call(edge_kernel, out_shape=[pltpu.VMEM((LANES, 3 * LANES), jnp...  2.91 us
    pallas_call x1, Pallas kernels, local(): pl.pallas_call(ice_kernel, out_shape=[struct(*ice), struct(2 * SOURCES, L...  2.65 us
    ppermute x1, starting transfers between devices, local(): below = near(lax.ppermute(up, 'face', ring('face', 1)))  2.11 us
    pallas_call x1, Pallas kernels, local(): pl.pallas_call(last_kernel, out_shape=[struct(LEVELS, ROWS, LANES), struc...  1.55 us
  transfers between devices with their start and end apart: 6, of which 3 were waited for; matrix products, arithmetic and copies ran while one was open for 0% of the time, Pallas kernels for 9%

commit v1 on v0

--- a/solution.py
+++ b/solution.py
@@ -172,8 +172,8 @@
 
 
 def look_up(tables, index):
-    high = index // LANES
-    low = index % LANES
+    high = index >> 7
+    low = index & (LANES - 1)
     found = [None] * len(tables)
     for row in range(len(tables[0])):
         here = high == row
@@ -274,8 +274,8 @@
     def step(block, total):
         start = pl.multiple_of(block * group, group)
         index = index_ref[pl.ds(start, group), :]
-        high = index // low_count
-        low = index % low_count
+        high = index >> (low_count.bit_length() - 1)
+        low = index & (low_count - 1)
         parts = [part for value in range(values) for part in in_three(read(value, start, group))]
         carried, spread = [], []
         for row in range(group):

time: 53.5 us -> 53.6 us (level)
  no operation moved by 1% of the time
where the time goes in v1:
time: 53.6 us; the launch traced here: 53.2 us
  starting transfers between devices  23 us (43%)
  waiting for transfers between devices  17.9 us (33%)
  Pallas kernels  11.7 us (22%)
  between operations  0.7 us (1%)
    all_to_all x2, waiting for transfers between devices, exchanged(): lax.all_to_all(blocks, BOTH, split_axis=0, concat_axis=0, tiled=True)  16.6 us
    all_to_all x2, starting transfers between devices, exchanged(): lax.all_to_all(blocks, BOTH, split_axis=0, concat_axis=0, tiled=True)  12.9 us
    ppermute x1, starting transfers between devices, local(): twin = near(lax.ppermute(sides, 'tile', swaps('tile', 0)))  3.35 us
    ppermute x1, starting transfers between devices, local(): cross = near(lax.ppermute(sides, 'tile', swaps('tile', 1)))  3.29 us
    pallas_call x1, Pallas kernels, local(): pl.pallas_call(edge_kernel, out_shape=[pltpu.VMEM((LANES, 3 * LANES), jnp...  2.91 us
    pallas_call x1, Pallas kernels, local(): pl.pallas_call(ice_kernel, out_shape=[struct(*ice), struct(2 * SOURCES, L...  2.7 us
    ppermute x1, starting transfers between devices, local(): below = near(lax.ppermute(up, 'face', ring('face', 1)))  2.11 us
    pallas_call x1, Pallas kernels, local(): pl.pallas_call(last_kernel, out_shape=[struct(LEVELS, ROWS, LANES), struc...  1.52 us
  transfers between devices with their start and end apart: 6, of which 3 were waited for; matrix products, arithmetic and copies ran while one was open for 0% of the time, Pallas kernels for 9%

profile of v1, /device:TPU:1, one launch (start us, length us, event | category | flops | bytes accessed | tf_op | source)
XLA Modules:
  0.0 53.2 jit_solution(4078557903062931225)
XLA Ops:
  0.6 1.0 %shard_map.165 = (f32[8,8,128]{2,1,0:T(8,128)S(1)}, f32[8,8,128]{2,1,0:T(8,128)S(1)}, f32[8,8,128]{2,1,0:T(8,128)S(1)}, f32[16,128]{1,0:T(8,128)S(1)}, f32[16,12...) custom-call(f32[8,8,128]{2,1,0:T(8,128)} %refs_0_.2, ...), custom_call_target="tpu_custom_call" | custom-call | tf_op jit(solution)/shard_map/pallas_call | solution.py:578
  1.7 2.1 %collective-permute-start.1 = (f32[48,128]{1,0:T(8,128)S(1)}, f32[48,128]{1,0:T(8,128)S(1)}, u32[]{:S(2)}, u32[]{:S(2)}) collective-permute-start(f32[48,128]{1,0:T(8,128)S(1)} %get-tuple-element.42), channel_id=1, source_target_pairs={{0,32},{32,64},{64,96},{96,0},{1,33},{33,65},{65,97},{97,1},{2,34}... | collective-permute-start | bytes 73736 | tf_op jit(solution)/shard_map/ppermute | solution.py:604
  3.8 1.3 %collective-permute-start = (f32[40,128]{1,0:T(8,128)S(1)}, f32[40,128]{1,0:T(8,128)S(1)}, u32[]{:S(2)}, u32[]{:S(2)}) collective-permute-start(f32[40,128]{1,0:T(8,128)S(1)} %get-tuple-element.41), channel_id=1, source_target_pairs={{0,96},{32,0},{64,32},{96,64},{1,97},{33,1},{65,33},{97,65},{2,98}... | collective-permute-start | bytes 61448 | tf_op jit(solution)/shard_map/ppermute | solution.py:603
  5.1 1.3 %collective-permute-done.above_ref = f32[40,128]{1,0:T(8,128)S(1)} collective-permute-done((f32[40,128]{1,0:T(8,128)S(1)}, f32[40,128]{1,0:T(8,128)S(1)}, u32[]{:S(2)}, u32[]{:S(2)}) %collective-permute-start) | collective-permute-done | bytes 20512 | tf_op jit(solution)/shard_map/ppermute | solution.py:603
  6.4 0.0 collective-permute-done.1.below_ref
  6.4 3.3 %collective-permute-start.3 = (f32[16,128]{1,0:T(8,128)S(1)}, f32[16,128]{1,0:T(8,128)S(1)}, u32[]{:S(2)}, u32[]{:S(2)}) collective-permute-start(f32[16,128]{1,0:T(8,128)S(1)} %shard_map.168), channel_id=1, source_target_pairs={{0,31},{1,2},{2,1},{3,4},{4,3},{5,6},{6,5},{7,8},{8,7},{9,10},{10,... | collective-permute-start | bytes 24584 | tf_op jit(solution)/shard_map/ppermute | solution.py:612
  9.7 3.4 %collective-permute-start.2 = (f32[16,128]{1,0:T(8,128)S(1)}, f32[16,128]{1,0:T(8,128)S(1)}, u32[]{:S(2)}, u32[]{:S(2)}) collective-permute-start(f32[16,128]{1,0:T(8,128)S(1)} %shard_map.168), channel_id=1, source_target_pairs={{0,1},{1,0},{2,3},{3,2},{4,5},{5,4},{6,7},{7,6},{8,9},{9,8},{10,11... | collective-permute-start | bytes 24584 | tf_op jit(solution)/shard_map/ppermute | solution.py:611
  13.1 1.2 %shard_map.166 = (f32[8,8,128]{2,1,0:T(8,128)S(1)}, s32[128,128]{1,0:T(8,128)S(1)}, f32[128,128]{1,0:T(8,128)S(1)}, f32[8,8,128]{2,1,0:T(8,128)S(1)}, s32[128,12...) custom-call(f32[8]{0:T(128)} %refs_0_.3, ...), custom_call_target="tpu_custom_call" | custom-call | tf_op jit(solution)/shard_map/pallas_call | solution.py:589
  14.3 0.0 collective-permute-done.3.cross_ref
  14.4 0.0 collective-permute-done.2.twin_ref
  14.4 1.5 %shard_map.169 = (f32[8,8,128]{2,1,0:T(8,128)}, f32[8,8,128]{2,1,0:T(8,128)S(1)}, f32[8,128]{1,0:T(8,128)S(1)}, f32[384,128]{1,0:T(8,128)}) custom-call(f32[8,128]{1,0:T(8,128)S(1)} %get-tuple-element.37.speed_ref, f32[24,16,128]{2,1,0:T(8,128)S(1)} %shard_map.167.wide_ref, f32[8,8,128]{2,1,0:T(8,128)S(1)} %get-tuple-element.43.heat_ref, ...), custom_call_target="tpu_custom_call" | custom-call | tf_op jit(solution)/shard_map/pallas_call | solution.py:613
  15.8 8.4 %all-to-all-start = ((f32[128,3,1,128]{3,2,1,0:T(1,128)}), f32[128,3,1,128]{3,2,1,0:T(1,128)S(1)}, u32[]{:S(2)}, u32[]{:S(2)}) async-start(f32[128,3,1,128]{3,2,1,0:T(1,128)} %bitcast.18), calls=%async_computation | async-start | bytes 393216 | tf_op jit(solution)/shard_map/all_to_all | solution.py:539
  24.2 2.9 %shard_map.170 = (bf16[128,384]{1,0:T(8,128)(2,1)S(1)}, f32[8,8,128]{2,1,0:T(8,128)S(1)}) custom-call(f32[16,128]{1,0:T(8,128)S(1)} %get-tuple-element.53.resist_ref, s32[16,128]{1,0:T(8,128)S(1)} %get-tuple-element.52.frozen_ref, f32[8,128]{1,0:T(8,128)S(1)} %get-tuple-element.54.halo_ref, f32[8,8,128]{2,1,0:T(8,128)S(1)} %get-tuple-element.55.gain_ref, ...), custom_call_target="tpu_custom_call" | custom-call | tf_op jit(solution)/shard_map/pallas_call | solution.py:636
  27.1 7.5 %all-to-all-done = f32[128,3,1,128]{3,2,1,0:T(1,128)S(1)} async-done(((f32[128,3,1,128]{3,2,1,0:T(1,128)}), f32[128,3,1,128]{3,2,1,0:T(1,128)S(1)}, u32[]{:S(2)}, u32[]{:S(2)}) %all-to-all-start) | async-done | bytes 196640 | tf_op jit(solution)/shard_map/all_to_all | solution.py:539
  34.6 2.7 %shard_map.171 = (f32[16,128]{1,0:T(8,128)}, f32[256,128]{1,0:T(8,128)}, f32[2,16,128]{2,1,0:T(8,128)S(1)}) custom-call(f32[384,128]{1,0:T(8,128)S(1)} %bitcast.16, s32[128,128]{1,0:T(8,128)S(1)} %get-tuple-element.50.target_ref, f32[16,128]{1,0:T(8,128)S(1)} %get-tuple-element.51.skin_ref, s32[16,128]{1,0:T(8,128)S(1)} %get-tuple-element.52.frozen_ref, ...), custom_call_target="tpu_custom_call" | custom-call | tf_op jit(solution)/shard_map/pallas_call | solution.py:644
  37.3 4.5 %all-to-all-start.1 = ((f32[128,2,1,128]{3,1,2,0:T(2,128)}), f32[128,2,1,128]{3,1,2,0:T(2,128)S(1)}, u32[]{:S(2)}, u32[]{:S(2)}) async-start(f32[128,2,1,128]{3,1,2,0:T(2,128)} %bitcast.19), calls=%async_computation.1 | async-start | bytes 262144 | tf_op jit(solution)/shard_map/all_to_all | solution.py:539
  41.8 0.8 %shard_map.172.drift_ref = f32[16,128]{1,0:T(8,128)S(1)} custom-call(f32[16,128]{1,0:T(8,128)S(1)} %get-tuple-element.61.motion_ref, f32[16,128]{1,0:T(8,128)S(1)} %get-tuple-element.62.strain_ref, f32[2,16,128]{2,1,0:T(8,128)S(1)} %get-tuple-element.63.ice_ref, f32[8,128]{1,0:T(8,128)S(1)} %get-tuple-element.54.halo_ref), custom_call_target="tpu_custom_call" | custom-call | tf_op jit(solution)/shard_map/pallas_call | solution.py:651
  42.6 9.2 %all-to-all-done.1 = f32[128,2,1,128]{3,1,2,0:T(2,128)S(1)} async-done(((f32[128,2,1,128]{3,1,2,0:T(2,128)}), f32[128,2,1,128]{3,1,2,0:T(2,128)S(1)}, u32[]{:S(2)}, u32[]{:S(2)}) %all-to-all-start.1) | async-done | bytes 131104 | tf_op jit(solution)/shard_map/all_to_all | solution.py:539
  51.7 1.5 %shard_map.173 = (f32[8,8,128]{2,1,0:T(8,128)}, f32[16,128]{1,0:T(8,128)}) custom-call(f32[256,128]{1,0:T(8,128)S(1)} %bitcast.17, s32[128,128]{1,0:T(8,128)S(1)} %get-tuple-element.45.site_ref, f32[8,8,128]{2,1,0:T(8,128)S(1)} %get-tuple-element.59.answer_ref, f32[8,8,128]{2,1,0:T(8,128)S(1)} %get-tuple-element.60.calm_ref, ...), custom_call_target="tpu_custom_call" | custom-call | tf_op jit(solution)/shard_map/pallas_call | solution.py:658
  (2 shorter events, 0.0 us)
Async XLA Ops:
  1.7 4.7 %collective-permute-start.1 = (f32[48,128]{1,0:T(8,128)S(1)}, f32[48,128]{1,0:T(8,128)S(1)}, u32[]{:S(2)}, u32[]{:S(2)}) collective-permute-start(f32[48,128]{1,0:T(8,128)S(1)} %get-tuple-element.42), channel_id=1, source_target_pairs={{0,32},{32,64},{64,96},{96,0},{1,33},{33,65},{65,97},{97,1},{2,34}... | collective-permute-start | bytes 73736 | tf_op jit(solution)/shard_map/ppermute | solution.py:604
  3.8 2.6 %collective-permute-start = (f32[40,128]{1,0:T(8,128)S(1)}, f32[40,128]{1,0:T(8,128)S(1)}, u32[]{:S(2)}, u32[]{:S(2)}) collective-permute-start(f32[40,128]{1,0:T(8,128)S(1)} %get-tuple-element.41), channel_id=1, source_target_pairs={{0,96},{32,0},{64,32},{96,64},{1,97},{33,1},{65,33},{97,65},{2,98}... | collective-permute-start | bytes 61448 | tf_op jit(solution)/shard_map/ppermute | solution.py:603
  6.4 7.9 %collective-permute-start.3 = (f32[16,128]{1,0:T(8,128)S(1)}, f32[16,128]{1,0:T(8,128)S(1)}, u32[]{:S(2)}, u32[]{:S(2)}) collective-permute-start(f32[16,128]{1,0:T(8,128)S(1)} %shard_map.168), channel_id=1, source_target_pairs={{0,31},{1,2},{2,1},{3,4},{4,3},{5,6},{6,5},{7,8},{8,7},{9,10},{10,... | collective-permute-start | bytes 24584 | tf_op jit(solution)/shard_map/ppermute | solution.py:612
  9.7 4.6 %collective-permute-start.2 = (f32[16,128]{1,0:T(8,128)S(1)}, f32[16,128]{1,0:T(8,128)S(1)}, u32[]{:S(2)}, u32[]{:S(2)}) collective-permute-start(f32[16,128]{1,0:T(8,128)S(1)} %shard_map.168), channel_id=1, source_target_pairs={{0,1},{1,0},{2,3},{3,2},{4,5},{5,4},{6,7},{7,6},{8,9},{9,8},{10,11... | collective-permute-start | bytes 24584 | tf_op jit(solution)/shard_map/ppermute | solution.py:611
  15.8 18.8 %all-to-all-start = ((f32[128,3,1,128]{3,2,1,0:T(1,128)}), f32[128,3,1,128]{3,2,1,0:T(1,128)S(1)}, u32[]{:S(2)}, u32[]{:S(2)}) async-start(f32[128,3,1,128]{3,2,1,0:T(1,128)} %bitcast.18), calls=%async_computation | async-start | bytes 393216 | tf_op jit(solution)/shard_map/all_to_all | solution.py:539
  37.3 14.4 %all-to-all-start.1 = ((f32[128,2,1,128]{3,1,2,0:T(2,128)}), f32[128,2,1,128]{3,1,2,0:T(2,128)S(1)}, u32[]{:S(2)}, u32[]{:S(2)}) async-start(f32[128,2,1,128]{3,1,2,0:T(2,128)} %bitcast.19), calls=%async_computation.1 | async-start | bytes 262144 | tf_op jit(solution)/shard_map/all_to_all | solution.py:539

commit v2 on v1

--- a/solution.py
+++ b/solution.py
@@ -250,9 +250,9 @@
         slots_out[pl.ds(3 * start + 2, ROWS, stride=3), :] = area_ref[here, :] * found[1]
     before = jnp.where(place == 0, left[11:12], left[10:11])
     after = jnp.where(place == TILES - 1, right[12:13], right[10:11])
-    for at in range(3):
-        halo_out[pl.ds(at, 1), :] = pltpu.roll(before, LANES - EVP - EVP * at, 1)
-        halo_out[pl.ds(4 + at, 1), :] = pltpu.roll(after, LANES - EVP * (at + 3), 1)
+    halo_out[pl.ds(0, 1), :] = before
+    halo_out[pl.ds(1, 1), :] = after
+    halo_out[pl.ds(2, 6), :] = jnp.zeros((6, LANES), jnp.float32)
 
 
 def in_three(values):
@@ -440,8 +440,15 @@
 
 
 def edge_kernel(
-    resist_ref, frozen_ref, halo_ref, gain_ref, rest_ref, out_ref, calm_out, held
+    resist_ref, frozen_ref, ends_ref, gain_ref, rest_ref, out_ref, calm_out, halo_out, held
 ):
+    halo = [None] * 8
+    for at in range(3):
+        halo[at] = pltpu.roll(ends_ref[0:1], LANES - EVP - EVP * at, 1)
+        halo[4 + at] = pltpu.roll(ends_ref[1:2], LANES - EVP * (at + 3), 1)
+    halo[3] = halo[7] = jnp.zeros((1, LANES), jnp.float32)
+    for at, row in enumerate(halo):
+        halo_out[pl.ds(at, 1), :] = row
     calm_out[LEVELS - 1] = calm = rest_ref[LEVELS - 1]
     for level in range(LEVELS - 2, -1, -1):
         calm = gain_ref[level] * calm + rest_ref[level]
@@ -455,8 +462,8 @@
         for row in (0, ICE_ROWS - 1)
     ]
     strength = (
-        jnp.where(here, ends[0], halo_ref[2:3]),
-        jnp.where(here, halo_ref[6:7], ends[1]),
+        jnp.where(here, ends[0], halo[2]),
+        jnp.where(here, halo[6], ends[1]),
     )
     pull = jnp.concatenate(
         [jnp.broadcast_to(pltpu.roll(row, half, 1), (24, LANES)) for row in strength], axis=0
@@ -633,11 +640,11 @@
         cross,
     )
     arrived = exchanged(slots, 3)
-    edge, calm = pl.pallas_call(
+    edge, calm, halo = pl.pallas_call(
         edge_kernel,
-        out_shape=[pltpu.VMEM((LANES, 3 * LANES), jnp.bfloat16), kept(LEVELS, ROWS, LANES)],
+        out_shape=[pltpu.VMEM((LANES, 3 * LANES), jnp.bfloat16), kept(LEVELS, ROWS, LANES), kept(8, LANES)],
         in_specs=[VMEM] * 5,
-        out_specs=[VMEM] * 2,
+        out_specs=[VMEM] * 3,
         scratch_shapes=[pltpu.VMEM((LANES, LANES), jnp.float32)],
     )(at["resist"], at["frozen"], near(halo), near(gain), near(rest))
     edge = near(edge)

time: 53.6 us -> 53.6 us (level)
  no operation moved by 1% of the time
where the time goes in v2:
time: 53.6 us; the launch traced here: 53.3 us
  starting transfers between devices  23 us (43%)
  waiting for transfers between devices  17.8 us (33%)
  Pallas kernels  11.8 us (22%)
  between operations  0.7 us (1%)
    all_to_all x2, waiting for transfers between devices, exchanged(): lax.all_to_all(blocks, BOTH, split_axis=0, concat_axis=0, tiled=True)  16.5 us
    all_to_all x2, starting transfers between devices, exchanged(): lax.all_to_all(blocks, BOTH, split_axis=0, concat_axis=0, tiled=True)  12.9 us
    ppermute x1, starting transfers between devices, local(): twin = near(lax.ppermute(sides, 'tile', swaps('tile', 0)))  3.35 us
    ppermute x1, starting transfers between devices, local(): cross = near(lax.ppermute(sides, 'tile', swaps('tile', 1)))  3.29 us
    pallas_call x1, Pallas kernels, local(): pl.pallas_call(edge_kernel, out_shape=[pltpu.VMEM((LANES, 3 * LANES), jnp...  2.98 us
    pallas_call x1, Pallas kernels, local(): pl.pallas_call(ice_kernel, out_shape=[struct(*ice), struct(2 * SOURCES, L...  2.7 us
    ppermute x1, starting transfers between devices, local(): below = near(lax.ppermute(up, 'face', ring('face', 1)))  2.11 us
    pallas_call x1, Pallas kernels, local(): pl.pallas_call(last_kernel, out_shape=[struct(LEVELS, ROWS, LANES), struc...  1.52 us
  transfers between devices with their start and end apart: 6, of which 3 were waited for; matrix products, arithmetic and copies ran while one was open for 0% of the time, Pallas kernels for 9%

profile of v2, /device:TPU:1, one launch (start us, length us, event | category | flops | bytes accessed | tf_op | source)
XLA Modules:
  0.0 53.3 jit_solution(1691017020686751618)
XLA Ops:
  0.6 1.0 %shard_map.165 = (f32[8,8,128]{2,1,0:T(8,128)S(1)}, f32[8,8,128]{2,1,0:T(8,128)S(1)}, f32[8,8,128]{2,1,0:T(8,128)S(1)}, f32[16,128]{1,0:T(8,128)S(1)}, f32[16,12...) custom-call(f32[8,8,128]{2,1,0:T(8,128)} %refs_0_.2, ...), custom_call_target="tpu_custom_call" | custom-call | tf_op jit(solution)/shard_map/pallas_call | solution.py:585
  1.7 2.1 %collective-permute-start.1 = (f32[48,128]{1,0:T(8,128)S(1)}, f32[48,128]{1,0:T(8,128)S(1)}, u32[]{:S(2)}, u32[]{:S(2)}) collective-permute-start(f32[48,128]{1,0:T(8,128)S(1)} %get-tuple-element.43), channel_id=1, source_target_pairs={{0,32},{32,64},{64,96},{96,0},{1,33},{33,65},{65,97},{97,1},{2,34}... | collective-permute-start | bytes 73736 | tf_op jit(solution)/shard_map/ppermute | solution.py:611
  3.8 1.3 %collective-permute-start = (f32[40,128]{1,0:T(8,128)S(1)}, f32[40,128]{1,0:T(8,128)S(1)}, u32[]{:S(2)}, u32[]{:S(2)}) collective-permute-start(f32[40,128]{1,0:T(8,128)S(1)} %get-tuple-element.42), channel_id=1, source_target_pairs={{0,96},{32,0},{64,32},{96,64},{1,97},{33,1},{65,33},{97,65},{2,98}... | collective-permute-start | bytes 61448 | tf_op jit(solution)/shard_map/ppermute | solution.py:610
  5.1 1.3 %collective-permute-done.above_ref = f32[40,128]{1,0:T(8,128)S(1)} collective-permute-done((f32[40,128]{1,0:T(8,128)S(1)}, f32[40,128]{1,0:T(8,128)S(1)}, u32[]{:S(2)}, u32[]{:S(2)}) %collective-permute-start) | collective-permute-done | bytes 20512 | tf_op jit(solution)/shard_map/ppermute | solution.py:610
  6.4 0.0 collective-permute-done.1.below_ref
  6.4 3.3 %collective-permute-start.3 = (f32[16,128]{1,0:T(8,128)S(1)}, f32[16,128]{1,0:T(8,128)S(1)}, u32[]{:S(2)}, u32[]{:S(2)}) collective-permute-start(f32[16,128]{1,0:T(8,128)S(1)} %shard_map.168), channel_id=1, source_target_pairs={{0,31},{1,2},{2,1},{3,4},{4,3},{5,6},{6,5},{7,8},{8,7},{9,10},{10,... | collective-permute-start | bytes 24584 | tf_op jit(solution)/shard_map/ppermute | solution.py:619
  9.7 3.4 %collective-permute-start.2 = (f32[16,128]{1,0:T(8,128)S(1)}, f32[16,128]{1,0:T(8,128)S(1)}, u32[]{:S(2)}, u32[]{:S(2)}) collective-permute-start(f32[16,128]{1,0:T(8,128)S(1)} %shard_map.168), channel_id=1, source_target_pairs={{0,1},{1,0},{2,3},{3,2},{4,5},{5,4},{6,7},{7,6},{8,9},{9,8},{10,11... | collective-permute-start | bytes 24584 | tf_op jit(solution)/shard_map/ppermute | solution.py:618
  13.1 1.2 %shard_map.166 = (f32[8,8,128]{2,1,0:T(8,128)S(1)}, s32[128,128]{1,0:T(8,128)S(1)}, f32[128,128]{1,0:T(8,128)S(1)}, f32[8,8,128]{2,1,0:T(8,128)S(1)}, s32[128,12...) custom-call(f32[8]{0:T(128)} %refs_0_.3, ...), custom_call_target="tpu_custom_call" | custom-call | tf_op jit(solution)/shard_map/pallas_call | solution.py:596
  14.3 0.0 collective-permute-done.3.cross_ref
  14.4 0.0 collective-permute-done.2.twin_ref
  14.4 1.5 %shard_map.169 = (f32[8,8,128]{2,1,0:T(8,128)}, f32[8,8,128]{2,1,0:T(8,128)S(1)}, f32[8,128]{1,0:T(8,128)S(1)}, f32[384,128]{1,0:T(8,128)}) custom-call(f32[8,128]{1,0:T(8,128)S(1)} %get-tuple-element.38.speed_ref, f32[24,16,128]{2,1,0:T(8,128)S(1)} %shard_map.167.wide_ref, f32[8,8,128]{2,1,0:T(8,128)S(1)} %get-tuple-element.44.heat_ref, ...), custom_call_target="tpu_custom_call" | custom-call | tf_op jit(solution)/shard_map/pallas_call | solution.py:620
  15.8 8.4 %all-to-all-start = ((f32[128,3,1,128]{3,2,1,0:T(1,128)}), f32[128,3,1,128]{3,2,1,0:T(1,128)S(1)}, u32[]{:S(2)}, u32[]{:S(2)}) async-start(f32[128,3,1,128]{3,2,1,0:T(1,128)} %bitcast.18), calls=%async_computation | async-start | bytes 393216 | tf_op jit(solution)/shard_map/all_to_all | solution.py:546
  24.2 3.0 %shard_map.170 = (bf16[128,384]{1,0:T(8,128)(2,1)S(1)}, f32[8,8,128]{2,1,0:T(8,128)S(1)}, f32[8,128]{1,0:T(8,128)S(1)}) custom-call(f32[16,128]{1,0:T(8,128)S(1)} %get-tuple-element.54.resist_ref, s32[16,128]{1,0:T(8,128)S(1)} %get-tuple-element.53.frozen_ref, f32[8,128]{1,0:T(8,128)S(1)} %get-tuple-element.55.ends_ref, ...), custom_call_target="tpu_custom_call" | custom-call | tf_op jit(solution)/shard_map/pallas_call | solution.py:643
  27.2 7.4 %all-to-all-done = f32[128,3,1,128]{3,2,1,0:T(1,128)S(1)} async-done(((f32[128,3,1,128]{3,2,1,0:T(1,128)}), f32[128,3,1,128]{3,2,1,0:T(1,128)S(1)}, u32[]{:S(2)}, u32[]{:S(2)}) %all-to-all-start) | async-done | bytes 196640 | tf_op jit(solution)/shard_map/all_to_all | solution.py:546
  34.6 2.7 %shard_map.171 = (f32[16,128]{1,0:T(8,128)}, f32[256,128]{1,0:T(8,128)}, f32[2,16,128]{2,1,0:T(8,128)S(1)}) custom-call(f32[384,128]{1,0:T(8,128)S(1)} %bitcast.16, s32[128,128]{1,0:T(8,128)S(1)} %get-tuple-element.51.target_ref, f32[16,128]{1,0:T(8,128)S(1)} %get-tuple-element.52.skin_ref, s32[16,128]{1,0:T(8,128)S(1)} %get-tuple-element.53.frozen_ref, ...), custom_call_target="tpu_custom_call" | custom-call | tf_op jit(solution)/shard_map/pallas_call | solution.py:651
  37.3 4.5 %all-to-all-start.1 = ((f32[128,2,1,128]{3,1,2,0:T(2,128)}), f32[128,2,1,128]{3,1,2,0:T(2,128)S(1)}, u32[]{:S(2)}, u32[]{:S(2)}) async-start(f32[128,2,1,128]{3,1,2,0:T(2,128)} %bitcast.19), calls=%async_computation.1 | async-start | bytes 262144 | tf_op jit(solution)/shard_map/all_to_all | solution.py:546
  41.8 0.8 %shard_map.172.drift_ref = f32[16,128]{1,0:T(8,128)S(1)} custom-call(f32[16,128]{1,0:T(8,128)S(1)} %get-tuple-element.62.motion_ref, f32[16,128]{1,0:T(8,128)S(1)} %get-tuple-element.63.strain_ref, f32[2,16,128]{2,1,0:T(8,128)S(1)} %get-tuple-element.64.ice_ref, f32[8,128]{1,0:T(8,128)S(1)} %get-tuple-element.65.halo_ref), custom_call_target="tpu_custom_call" | custom-call | tf_op jit(solution)/shard_map/pallas_call | solution.py:658
  42.6 9.2 %all-to-all-done.1 = f32[128,2,1,128]{3,1,2,0:T(2,128)S(1)} async-done(((f32[128,2,1,128]{3,1,2,0:T(2,128)}), f32[128,2,1,128]{3,1,2,0:T(2,128)S(1)}, u32[]{:S(2)}, u32[]{:S(2)}) %all-to-all-start.1) | async-done | bytes 131104 | tf_op jit(solution)/shard_map/all_to_all | solution.py:546
  51.7 1.5 %shard_map.173 = (f32[8,8,128]{2,1,0:T(8,128)}, f32[16,128]{1,0:T(8,128)}) custom-call(f32[256,128]{1,0:T(8,128)S(1)} %bitcast.17, s32[128,128]{1,0:T(8,128)S(1)} %get-tuple-element.46.site_ref, f32[8,8,128]{2,1,0:T(8,128)S(1)} %get-tuple-element.60.answer_ref, f32[8,8,128]{2,1,0:T(8,128)S(1)} %get-tuple-element.61.calm_ref, ...), custom_call_target="tpu_custom_call" | custom-call | tf_op jit(solution)/shard_map/pallas_call | solution.py:665
  (2 shorter events, 0.0 us)
Async XLA Ops:
  1.7 4.7 %collective-permute-start.1 = (f32[48,128]{1,0:T(8,128)S(1)}, f32[48,128]{1,0:T(8,128)S(1)}, u32[]{:S(2)}, u32[]{:S(2)}) collective-permute-start(f32[48,128]{1,0:T(8,128)S(1)} %get-tuple-element.43), channel_id=1, source_target_pairs={{0,32},{32,64},{64,96},{96,0},{1,33},{33,65},{65,97},{97,1},{2,34}... | collective-permute-start | bytes 73736 | tf_op jit(solution)/shard_map/ppermute | solution.py:611
  3.8 2.6 %collective-permute-start = (f32[40,128]{1,0:T(8,128)S(1)}, f32[40,128]{1,0:T(8,128)S(1)}, u32[]{:S(2)}, u32[]{:S(2)}) collective-permute-start(f32[40,128]{1,0:T(8,128)S(1)} %get-tuple-element.42), channel_id=1, source_target_pairs={{0,96},{32,0},{64,32},{96,64},{1,97},{33,1},{65,33},{97,65},{2,98}... | collective-permute-start | bytes 61448 | tf_op jit(solution)/shard_map/ppermute | solution.py:610
  6.4 7.9 %collective-permute-start.3 = (f32[16,128]{1,0:T(8,128)S(1)}, f32[16,128]{1,0:T(8,128)S(1)}, u32[]{:S(2)}, u32[]{:S(2)}) collective-permute-start(f32[16,128]{1,0:T(8,128)S(1)} %shard_map.168), channel_id=1, source_target_pairs={{0,31},{1,2},{2,1},{3,4},{4,3},{5,6},{6,5},{7,8},{8,7},{9,10},{10,... | collective-permute-start | bytes 24584 | tf_op jit(solution)/shard_map/ppermute | solution.py:619
  9.7 4.6 %collective-permute-start.2 = (f32[16,128]{1,0:T(8,128)S(1)}, f32[16,128]{1,0:T(8,128)S(1)}, u32[]{:S(2)}, u32[]{:S(2)}) collective-permute-start(f32[16,128]{1,0:T(8,128)S(1)} %shard_map.168), channel_id=1, source_target_pairs={{0,1},{1,0},{2,3},{3,2},{4,5},{5,4},{6,7},{7,6},{8,9},{9,8},{10,11... | collective-permute-start | bytes 24584 | tf_op jit(solution)/shard_map/ppermute | solution.py:618
  15.8 18.8 %all-to-all-start = ((f32[128,3,1,128]{3,2,1,0:T(1,128)}), f32[128,3,1,128]{3,2,1,0:T(1,128)S(1)}, u32[]{:S(2)}, u32[]{:S(2)}) async-start(f32[128,3,1,128]{3,2,1,0:T(1,128)} %bitcast.18), calls=%async_computation | async-start | bytes 393216 | tf_op jit(solution)/shard_map/all_to_all | solution.py:546
  37.3 14.4 %all-to-all-start.1 = ((f32[128,2,1,128]{3,1,2,0:T(2,128)}), f32[128,2,1,128]{3,1,2,0:T(2,128)S(1)}, u32[]{:S(2)}, u32[]{:S(2)}) async-start(f32[128,2,1,128]{3,1,2,0:T(2,128)} %bitcast.19), calls=%async_computation.1 | async-start | bytes 262144 | tf_op jit(solution)/shard_map/all_to_all | solution.py:546
